TPU v7x, 32 devices: a whole 2x2x4 slice. The times are simulated.
32 devices in a mesh: groups: 2 (over x), blk: 16 (over z, y, core).
Axes of the slice: x: 2, y: 2, z: 4, core: 2. Of those that a mesh axis runs over, the one named last changes fastest.
Arguments:
- grads: bfloat16 [192, 32768], P('groups', 'blk'), parts along dimension 0, may hold values from -6 to 6
- block_values: bfloat16 [4096, 128, 128], P('blk'), may hold values from -0.046875 to 0.046875
- block_rows: int32 [4096], P('blk'), may hold values from 0 to 15, as said below
- block_cols: int32 [4096], P('blk'), may hold values from 0 to 31
- block_counts: int32 [16], P('blk'), may hold values from 129 to 256, as said below
- inv_gram: bfloat16 [4096, 4096], P('blk'), may hold values from -0.09375 to 0.09375
- queries: bfloat16 [256, 4096], P(('groups', 'blk')), parts along dimension 0, may hold values from -0.09375 to 0.09375
Outputs:
- scores: float32 [192, 128], P(('groups', 'blk')), parts along dimension 0
There are 2 independent parts, one for each index of `groups`. A program takes and returns all parts, laid end to end along the dimension named above; an argument that names none is the same for every part. Nothing has to cross between parts.
Inputs may be any that keep to these rules, and one draw needn't show every extreme that they name: `block_rows`: the slots of one parameter block name distinct pairs of block row and block column. The first block_counts[d] slots of parameter block d are used; some parameter block uses all 256.
All inputs are finite; a program needn't handle non-finite values.
Results may differ from a plain program's by a relative error of at most 0.0029.
Values may be sent and summed in bfloat16 or wider, within the bound.
A program may use at most 128 MiB of HBM per device.

v0:
```python
import jax
import jax.numpy as jnp
from jax import lax
from jax.sharding import PartitionSpec as P


def passed_along(value, axis, by):
    devices = lax.axis_size(axis)
    return lax.ppermute(value, axis, [(i, (i + by) % devices) for i in range(devices)])


def cycle_tiles(moving, make_tile):
    cycle_size = lax.axis_size("blk")
    position = lax.axis_index("blk")
    first_tile = make_tile(moving)
    tile_stack = jnp.zeros((cycle_size,) + first_tile.shape, jnp.float32)
    tile_stack = lax.dynamic_update_index_in_dim(tile_stack, first_tile, position, 0)

    def advance_one(step_index, carry):
        stack_now, current = carry
        current = passed_along(current, "blk", 1)
        stack_now = lax.dynamic_update_index_in_dim(
            stack_now, make_tile(current), (position - step_index) % cycle_size, 0
        )
        return (stack_now, current)

    tile_stack = lax.fori_loop(1, cycle_size, advance_one, (tile_stack, moving))[0]
    return tile_stack


def shards(grads, block_values, block_rows, block_cols, block_counts, inv_gram, queries):
    examples, param_width = grads.shape
    slot_count = block_values.shape[0]
    block_side = block_values.shape[1]
    feature_dim = inv_gram.shape[1]
    col_blocks = feature_dim // block_side
    tiled = grads.reshape(examples, param_width // block_side, block_side)
    slot_group = 64
    group_count = slot_count // slot_group
    live_slots = (jnp.arange(slot_count, dtype=jnp.int32) < block_counts[0]).astype(jnp.bfloat16)

    def add_group(totals, inputs):
        group_rows, group_cols, group_values, group_live = inputs
        selected = jnp.take(tiled, group_rows, axis=1)
        weights = group_values * group_live[:, None, None]
        products = jnp.einsum("ejb,jbc->ejc", selected, weights, preferred_element_type=jnp.float32)
        return (totals.at[:, group_cols, :].add(products), None)

    group_inputs = (
        block_rows.reshape(group_count, slot_group),
        block_cols.reshape(group_count, slot_group),
        block_values.reshape(group_count, slot_group, block_side, block_side),
        live_slots.reshape(group_count, slot_group),
    )
    start_totals = jnp.zeros((examples, col_blocks, block_side), jnp.float32)
    totals, unused = lax.scan(add_group, start_totals, group_inputs)
    partial_features = totals.reshape(examples, feature_dim)
    contract = (((1,), (1,)), ((), ()))

    def tile_for_queries(query_block):
        return lax.dot_general(inv_gram, query_block, contract, preferred_element_type=jnp.float32)

    tile_stack = cycle_tiles(queries, tile_for_queries)
    gram_rows = inv_gram.shape[0]
    whitened_queries = (
        jnp.transpose(tile_stack, (1, 0, 2)).reshape(gram_rows, -1).astype(jnp.bfloat16)
    )
    features = lax.psum_scatter(partial_features, "blk", scatter_dimension=1, tiled=True)
    query_float = whitened_queries.astype(jnp.float32)
    return lax.psum_scatter(
        jnp.dot(features, query_float, precision=lax.Precision.HIGHEST),
        "blk",
        scatter_dimension=0,
        tiled=True,
    )


def solution(mesh):
    placed = (
        P("groups", "blk"),
        P("blk", None, None),
        P("blk"),
        P("blk"),
        P("blk"),
        P("blk", None),
        P(("groups", "blk"), None),
    )
    return jax.shard_map(
        shards, mesh=mesh, in_specs=placed, out_specs=P(("groups", "blk"), None), check_vma=False
    )
```

profile of v0, /device:TPU:0, one launch (start us, length us, event | category | flops | bytes accessed | tf_op | source)
XLA Modules:
  0.0 255.2 jit_solution(10742330173522169308)
XLA Ops:
  6.5 1.5 copy.38
  8.1 0.8 reshape.83
  9.5 0.8 reshape.85
  10.2 0.8 copy_bitcast_fusion.1
  11.0 1.3 broadcast_in_dim.32
  12.4 64.0 %while.27 = (s32[]{:T(128)}, f32[96,32,128]{2,0,1:T(8,128)}, s32[4,64]{1,0:T(4,128)S(1)}, bf16[4,64,128,128]{3,2,1,0:T(8,128)(2,1)}, bf16[4,64]{1,0:T(4,128)(2,1...) while((s32[]{:T(128)}, f32[96,32,128]{2,0,1:T(8,128)}, s32[4,64]{1,0:T(4,128)S(1)}, ...), condition=%wide.region_2.3_spmd, body=%wide.region_0.2_spmd.sunk | while | flops 203949824 | bytes 19405420 | solution.py:56
  12.4 2.9 %gather_fusion = bf16[64,96,128]{2,1,0:T(8,128)(2,1)} fusion(bf16[96,16,128]{2,0,1:T(8,128)(2,1)} %get-tuple-element.317, s32[1024]{0:T(1024)S(1)} %pad_clamp_fusion.2), kind=kCustom, calls=%fused_computation.clone.1 | custom fusion | bytes 3145984 | tf_op jit(solution)/shard_map/while/body/eval_jaxpr/jit(_take)/gather | solution.py:44
  15.4 2.8 %fusion.36 = f32[64,96,128]{2,1,0:T(8,128)S(1)} fusion(bf16[4,64,128,128]{3,2,1,0:T(8,128)(2,1)} %get-tuple-element.314, s32[]{:T(128)S(6)} %copy.22, bf16[64,96,128]{2,1,0:T(8,128)(2,1)} %gather_fusion, pred[64]{0:T(512)(128)(4,1)S(1)} %compare_and_fusion.2, bf16[64]{0:T(256)(128)(2,1)S(1)} %fusion.35), kind=kOutput, calls=%fused_computation.5.clone.1 | convolution fusion | flops 203161600 | bytes 6815940 | tf_op jit(solution)/shard_map/while/body/eval_jaxpr/ejb,jbc->ejc/dot_general | solution.py:46
  18.2 10.2 %scatter_fusion = f32[96,32,128]{2,0,1:T(8,128)} fusion(f32[96,32,128]{2,0,1:T(8,128)} %get-tuple-element.304, s32[64]{0:T(128)S(1)} %get-tuple-element.288, f32[64,96,128]{2,1,0:T(8,128)S(1)} %fusion.36), kind=kCustom, calls=%fused_computation.1.clone.1 | custom fusion | flops 786432 | bytes 9437440 | tf_op jit(solution)/shard_map/while/body/eval_jaxpr/scatter-add | solution.py:47
  28.4 2.9 %gather_fusion = bf16[64,96,128]{2,1,0:T(8,128)(2,1)} fusion(bf16[96,16,128]{2,0,1:T(8,128)(2,1)} %get-tuple-element.317, s32[1024]{0:T(1024)S(1)} %pad_clamp_fusion.2), kind=kCustom, calls=%fused_computation.clone.1 | custom fusion | bytes 3145984 | tf_op jit(solution)/shard_map/while/body/eval_jaxpr/jit(_take)/gather | solution.py:44
  31.4 2.8 %fusion.36 = f32[64,96,128]{2,1,0:T(8,128)S(1)} fusion(bf16[4,64,128,128]{3,2,1,0:T(8,128)(2,1)} %get-tuple-element.314, s32[]{:T(128)S(6)} %copy.22, bf16[64,96,128]{2,1,0:T(8,128)(2,1)} %gather_fusion, pred[64]{0:T(512)(128)(4,1)S(1)} %compare_and_fusion.2, bf16[64]{0:T(256)(128)(2,1)S(1)} %fusion.35), kind=kOutput, calls=%fused_computation.5.clone.1 | convolution fusion | flops 203161600 | bytes 6815940 | tf_op jit(solution)/shard_map/while/body/eval_jaxpr/ejb,jbc->ejc/dot_general | solution.py:46
  34.2 10.2 %scatter_fusion = f32[96,32,128]{2,0,1:T(8,128)} fusion(f32[96,32,128]{2,0,1:T(8,128)} %get-tuple-element.304, s32[64]{0:T(128)S(1)} %get-tuple-element.288, f32[64,96,128]{2,1,0:T(8,128)S(1)} %fusion.36), kind=kCustom, calls=%fused_computation.1.clone.1 | custom fusion | flops 786432 | bytes 9437440 | tf_op jit(solution)/shard_map/while/body/eval_jaxpr/scatter-add | solution.py:47
  44.4 2.9 %gather_fusion = bf16[64,96,128]{2,1,0:T(8,128)(2,1)} fusion(bf16[96,16,128]{2,0,1:T(8,128)(2,1)} %get-tuple-element.317, s32[1024]{0:T(1024)S(1)} %pad_clamp_fusion.2), kind=kCustom, calls=%fused_computation.clone.1 | custom fusion | bytes 3145984 | tf_op jit(solution)/shard_map/while/body/eval_jaxpr/jit(_take)/gather | solution.py:44
  47.4 2.8 %fusion.36 = f32[64,96,128]{2,1,0:T(8,128)S(1)} fusion(bf16[4,64,128,128]{3,2,1,0:T(8,128)(2,1)} %get-tuple-element.314, s32[]{:T(128)S(6)} %copy.22, bf16[64,96,128]{2,1,0:T(8,128)(2,1)} %gather_fusion, pred[64]{0:T(512)(128)(4,1)S(1)} %compare_and_fusion.2, bf16[64]{0:T(256)(128)(2,1)S(1)} %fusion.35), kind=kOutput, calls=%fused_computation.5.clone.1 | convolution fusion | flops 203161600 | bytes 6815940 | tf_op jit(solution)/shard_map/while/body/eval_jaxpr/ejb,jbc->ejc/dot_general | solution.py:46
  50.2 10.1 %scatter_fusion = f32[96,32,128]{2,0,1:T(8,128)} fusion(f32[96,32,128]{2,0,1:T(8,128)} %get-tuple-element.304, s32[64]{0:T(128)S(1)} %get-tuple-element.288, f32[64,96,128]{2,1,0:T(8,128)S(1)} %fusion.36), kind=kCustom, calls=%fused_computation.1.clone.1 | custom fusion | flops 786432 | bytes 9437440 | tf_op jit(solution)/shard_map/while/body/eval_jaxpr/scatter-add | solution.py:47
  60.4 2.9 %gather_fusion = bf16[64,96,128]{2,1,0:T(8,128)(2,1)} fusion(bf16[96,16,128]{2,0,1:T(8,128)(2,1)} %get-tuple-element.317, s32[1024]{0:T(1024)S(1)} %pad_clamp_fusion.2), kind=kCustom, calls=%fused_computation.clone.1 | custom fusion | bytes 3145984 | tf_op jit(solution)/shard_map/while/body/eval_jaxpr/jit(_take)/gather | solution.py:44
  63.3 2.8 %fusion.36 = f32[64,96,128]{2,1,0:T(8,128)S(1)} fusion(bf16[4,64,128,128]{3,2,1,0:T(8,128)(2,1)} %get-tuple-element.314, s32[]{:T(128)S(6)} %copy.22, bf16[64,96,128]{2,1,0:T(8,128)(2,1)} %gather_fusion, pred[64]{0:T(512)(128)(4,1)S(1)} %compare_and_fusion.2, bf16[64]{0:T(256)(128)(2,1)S(1)} %fusion.35), kind=kOutput, calls=%fused_computation.5.clone.1 | convolution fusion | flops 203161600 | bytes 6815940 | tf_op jit(solution)/shard_map/while/body/eval_jaxpr/ejb,jbc->ejc/dot_general | solution.py:46
  66.2 10.2 %scatter_fusion = f32[96,32,128]{2,0,1:T(8,128)} fusion(f32[96,32,128]{2,0,1:T(8,128)} %get-tuple-element.304, s32[64]{0:T(128)S(1)} %get-tuple-element.288, f32[64,96,128]{2,1,0:T(8,128)S(1)} %fusion.36), kind=kCustom, calls=%fused_computation.1.clone.1 | custom fusion | flops 786432 | bytes 9437440 | tf_op jit(solution)/shard_map/while/body/eval_jaxpr/scatter-add | solution.py:47
  76.4 2.9 %copy_bitcast_fusion = f32[96,4096]{1,0:T(8,128)} fusion(f32[96,32,128]{2,0,1:T(8,128)} %get-tuple-element.175), kind=kLoop, calls=%fused_computation.26 | loop fusion | bytes 3145728 | tf_op jit(solution)/shard_map/reshape | solution.py:57
  79.9 0.6 dynamic-slice
  81.3 0.6 fusion.14
  81.9 107.0 %while.28 = (s32[]{:T(128)}, bf16[16,256,8]{1,2,0:T(8,128)(2,1)S(1)}, bf16[8,4096]{1,0:T(8,128)(2,1)S(1)}, bf16[256,4096]{1,0:T(8,128)(2,1)S(1)}, s32[]{:T(128)}...) while((s32[]{:T(128)}, bf16[16,256,8]{1,2,0:T(8,128)(2,1)S(1)}, bf16[8,4096]{1,0:T(8,128)(2,1)S(1)}, ...), condition=%wide.region_5.6_spmd, body=%wide.region_4.5_spmd.sunk | while | flops 16777232 | bytes 2564388 | solution.py:27
  82.1 6.9 %collective-permute-done = bf16[8,4096]{1,0:T(8,128)(2,1)S(1)} collective-permute-done((bf16[8,4096]{1,0:T(8,128)(2,1)S(1)}, bf16[8,4096]{1,0:T(8,128)(2,1)S(1)}, u32[]{:S(2)}, u32[]{:S(2)}) %collective-permute-start) | collective-permute-done | bytes 65568 | tf_op jit(solution)/shard_map/while/body/eval_jaxpr/ppermute | solution.py:9
  89.1 0.6 fusion.39
  89.7 6.4 %collective-permute-done = bf16[8,4096]{1,0:T(8,128)(2,1)S(1)} collective-permute-done((bf16[8,4096]{1,0:T(8,128)(2,1)S(1)}, bf16[8,4096]{1,0:T(8,128)(2,1)S(1)}, u32[]{:S(2)}, u32[]{:S(2)}) %collective-permute-start) | collective-permute-done | bytes 65568 | tf_op jit(solution)/shard_map/while/body/eval_jaxpr/ppermute | solution.py:9
  96.1 0.6 fusion.39
  96.7 6.4 %collective-permute-done = bf16[8,4096]{1,0:T(8,128)(2,1)S(1)} collective-permute-done((bf16[8,4096]{1,0:T(8,128)(2,1)S(1)}, bf16[8,4096]{1,0:T(8,128)(2,1)S(1)}, u32[]{:S(2)}, u32[]{:S(2)}) %collective-permute-start) | collective-permute-done | bytes 65568 | tf_op jit(solution)/shard_map/while/body/eval_jaxpr/ppermute | solution.py:9
  103.1 0.6 fusion.39
  103.8 6.4 %collective-permute-done = bf16[8,4096]{1,0:T(8,128)(2,1)S(1)} collective-permute-done((bf16[8,4096]{1,0:T(8,128)(2,1)S(1)}, bf16[8,4096]{1,0:T(8,128)(2,1)S(1)}, u32[]{:S(2)}, u32[]{:S(2)}) %collective-permute-start) | collective-permute-done | bytes 65568 | tf_op jit(solution)/shard_map/while/body/eval_jaxpr/ppermute | solution.py:9
  110.2 0.6 fusion.39
  110.8 6.4 %collective-permute-done = bf16[8,4096]{1,0:T(8,128)(2,1)S(1)} collective-permute-done((bf16[8,4096]{1,0:T(8,128)(2,1)S(1)}, bf16[8,4096]{1,0:T(8,128)(2,1)S(1)}, u32[]{:S(2)}, u32[]{:S(2)}) %collective-permute-start) | collective-permute-done | bytes 65568 | tf_op jit(solution)/shard_map/while/body/eval_jaxpr/ppermute | solution.py:9
  117.3 0.6 fusion.39
  117.9 6.5 %collective-permute-done = bf16[8,4096]{1,0:T(8,128)(2,1)S(1)} collective-permute-done((bf16[8,4096]{1,0:T(8,128)(2,1)S(1)}, bf16[8,4096]{1,0:T(8,128)(2,1)S(1)}, u32[]{:S(2)}, u32[]{:S(2)}) %collective-permute-start) | collective-permute-done | bytes 65568 | tf_op jit(solution)/shard_map/while/body/eval_jaxpr/ppermute | solution.py:9
  124.4 0.6 fusion.39
  125.1 6.4 %collective-permute-done = bf16[8,4096]{1,0:T(8,128)(2,1)S(1)} collective-permute-done((bf16[8,4096]{1,0:T(8,128)(2,1)S(1)}, bf16[8,4096]{1,0:T(8,128)(2,1)S(1)}, u32[]{:S(2)}, u32[]{:S(2)}) %collective-permute-start) | collective-permute-done | bytes 65568 | tf_op jit(solution)/shard_map/while/body/eval_jaxpr/ppermute | solution.py:9
  132.1 6.8 %collective-permute-done = bf16[8,4096]{1,0:T(8,128)(2,1)S(1)} collective-permute-done((bf16[8,4096]{1,0:T(8,128)(2,1)S(1)}, bf16[8,4096]{1,0:T(8,128)(2,1)S(1)}, u32[]{:S(2)}, u32[]{:S(2)}) %collective-permute-start) | collective-permute-done | bytes 65568 | tf_op jit(solution)/shard_map/while/body/eval_jaxpr/ppermute | solution.py:9
  138.9 0.6 fusion.39
  139.5 6.4 %collective-permute-done = bf16[8,4096]{1,0:T(8,128)(2,1)S(1)} collective-permute-done((bf16[8,4096]{1,0:T(8,128)(2,1)S(1)}, bf16[8,4096]{1,0:T(8,128)(2,1)S(1)}, u32[]{:S(2)}, u32[]{:S(2)}) %collective-permute-start) | collective-permute-done | bytes 65568 | tf_op jit(solution)/shard_map/while/body/eval_jaxpr/ppermute | solution.py:9
  146.6 6.4 %collective-permute-done = bf16[8,4096]{1,0:T(8,128)(2,1)S(1)} collective-permute-done((bf16[8,4096]{1,0:T(8,128)(2,1)S(1)}, bf16[8,4096]{1,0:T(8,128)(2,1)S(1)}, u32[]{:S(2)}, u32[]{:S(2)}) %collective-permute-start) | collective-permute-done | bytes 65568 | tf_op jit(solution)/shard_map/while/body/eval_jaxpr/ppermute | solution.py:9
  153.6 6.4 %collective-permute-done = bf16[8,4096]{1,0:T(8,128)(2,1)S(1)} collective-permute-done((bf16[8,4096]{1,0:T(8,128)(2,1)S(1)}, bf16[8,4096]{1,0:T(8,128)(2,1)S(1)}, u32[]{:S(2)}, u32[]{:S(2)}) %collective-permute-start) | collective-permute-done | bytes 65568 | tf_op jit(solution)/shard_map/while/body/eval_jaxpr/ppermute | solution.py:9
  160.7 6.4 %collective-permute-done = bf16[8,4096]{1,0:T(8,128)(2,1)S(1)} collective-permute-done((bf16[8,4096]{1,0:T(8,128)(2,1)S(1)}, bf16[8,4096]{1,0:T(8,128)(2,1)S(1)}, u32[]{:S(2)}, u32[]{:S(2)}) %collective-permute-start) | collective-permute-done | bytes 65568 | tf_op jit(solution)/shard_map/while/body/eval_jaxpr/ppermute | solution.py:9
  167.1 0.6 fusion.39
  167.7 6.4 %collective-permute-done = bf16[8,4096]{1,0:T(8,128)(2,1)S(1)} collective-permute-done((bf16[8,4096]{1,0:T(8,128)(2,1)S(1)}, bf16[8,4096]{1,0:T(8,128)(2,1)S(1)}, u32[]{:S(2)}, u32[]{:S(2)}) %collective-permute-start) | collective-permute-done | bytes 65568 | tf_op jit(solution)/shard_map/while/body/eval_jaxpr/ppermute | solution.py:9
  174.8 6.4 %collective-permute-done = bf16[8,4096]{1,0:T(8,128)(2,1)S(1)} collective-permute-done((bf16[8,4096]{1,0:T(8,128)(2,1)S(1)}, bf16[8,4096]{1,0:T(8,128)(2,1)S(1)}, u32[]{:S(2)}, u32[]{:S(2)}) %collective-permute-start) | collective-permute-done | bytes 65568 | tf_op jit(solution)/shard_map/while/body/eval_jaxpr/ppermute | solution.py:9
  181.2 0.6 fusion.39
  181.8 6.4 %collective-permute-done = bf16[8,4096]{1,0:T(8,128)(2,1)S(1)} collective-permute-done((bf16[8,4096]{1,0:T(8,128)(2,1)S(1)}, bf16[8,4096]{1,0:T(8,128)(2,1)S(1)}, u32[]{:S(2)}, u32[]{:S(2)}) %collective-permute-start) | collective-permute-done | bytes 65568 | tf_op jit(solution)/shard_map/while/body/eval_jaxpr/ppermute | solution.py:9
  188.9 1.1 fusion.15
  190.0 57.7 %all-reduce = f32[96,128]{1,0:T(8,128)S(1)} all-reduce(f32[96,128]{1,0:T(8,128)S(1)} %fusion.15), channel_id=3, replica_groups=mesh['groups'=2,'blk'=16] {'blk'}, use_global_device_ids=true, to_apply=%region_6.7.clone | all-reduce | flops 12288 | bytes 98304
  (66 shorter events, 5.6 us)
Async XLA Ops:
  6.5 3.7 %copy-start = (bf16[96,2048]{1,0:T(8,128)(2,1)S(1)}, bf16[96,2048]{1,0:T(8,128)(2,1)}, u32[]{:S(2)}) copy-start(bf16[96,2048]{1,0:T(8,128)(2,1)} %param.11) | copy-start | bytes 1179652
  6.5 182.3 %reduce-scatter.2.cloned.1.call-start = ((), (), s32[]{:S(2)}) async-start(), calls=%async_computation.1 | async-start | bytes 1671168 | tf_op jit(solution)/shard_map/reduce_scatter | solution.py:68
  76.4 4.9 %copy-start.1 = (bf16[256,4096]{1,0:T(8,128)(2,1)S(1)}, bf16[256,4096]{1,0:T(8,128)(2,1)}, u32[]{:S(2)}) copy-start(bf16[256,4096]{1,0:T(8,128)(2,1)} %param.16) | copy-start | bytes 6291460
  79.3 0.7 copy-start.3
  79.3 2.0 copy-start.2
  81.9 7.1 %collective-permute-start = (bf16[8,4096]{1,0:T(8,128)(2,1)S(1)}, bf16[8,4096]{1,0:T(8,128)(2,1)S(1)}, u32[]{:S(2)}, u32[]{:S(2)}) collective-permute-start(bf16[8,4096]{1,0:T(8,128)(2,1)S(1)} %get-tuple-element.330), channel_id=1, source_target_pairs={{0,1},{1,2},{2,3},{3,4},{4,5},{5,6},{6,7},{7,8},{8,9},{9,10},{10,1... | collective-permute-start | bytes 196616 | tf_op jit(solution)/shard_map/while/body/eval_jaxpr/ppermute | solution.py:9
  89.7 6.4 %collective-permute-start = (bf16[8,4096]{1,0:T(8,128)(2,1)S(1)}, bf16[8,4096]{1,0:T(8,128)(2,1)S(1)}, u32[]{:S(2)}, u32[]{:S(2)}) collective-permute-start(bf16[8,4096]{1,0:T(8,128)(2,1)S(1)} %get-tuple-element.330), channel_id=1, source_target_pairs={{0,1},{1,2},{2,3},{3,4},{4,5},{5,6},{6,7},{7,8},{8,9},{9,10},{10,1... | collective-permute-start | bytes 196616 | tf_op jit(solution)/shard_map/while/body/eval_jaxpr/ppermute | solution.py:9
  96.7 6.4 %collective-permute-start = (bf16[8,4096]{1,0:T(8,128)(2,1)S(1)}, bf16[8,4096]{1,0:T(8,128)(2,1)S(1)}, u32[]{:S(2)}, u32[]{:S(2)}) collective-permute-start(bf16[8,4096]{1,0:T(8,128)(2,1)S(1)} %get-tuple-element.330), channel_id=1, source_target_pairs={{0,1},{1,2},{2,3},{3,4},{4,5},{5,6},{6,7},{7,8},{8,9},{9,10},{10,1... | collective-permute-start | bytes 196616 | tf_op jit(solution)/shard_map/while/body/eval_jaxpr/ppermute | solution.py:9
  103.8 6.4 %collective-permute-start = (bf16[8,4096]{1,0:T(8,128)(2,1)S(1)}, bf16[8,4096]{1,0:T(8,128)(2,1)S(1)}, u32[]{:S(2)}, u32[]{:S(2)}) collective-permute-start(bf16[8,4096]{1,0:T(8,128)(2,1)S(1)} %get-tuple-element.330), channel_id=1, source_target_pairs={{0,1},{1,2},{2,3},{3,4},{4,5},{5,6},{6,7},{7,8},{8,9},{9,10},{10,1... | collective-permute-start | bytes 196616 | tf_op jit(solution)/shard_map/while/body/eval_jaxpr/ppermute | solution.py:9
  110.8 6.4 %collective-permute-start = (bf16[8,4096]{1,0:T(8,128)(2,1)S(1)}, bf16[8,4096]{1,0:T(8,128)(2,1)S(1)}, u32[]{:S(2)}, u32[]{:S(2)}) collective-permute-start(bf16[8,4096]{1,0:T(8,128)(2,1)S(1)} %get-tuple-element.330), channel_id=1, source_target_pairs={{0,1},{1,2},{2,3},{3,4},{4,5},{5,6},{6,7},{7,8},{8,9},{9,10},{10,1... | collective-permute-start | bytes 196616 | tf_op jit(solution)/shard_map/while/body/eval_jaxpr/ppermute | solution.py:9
  117.9 6.5 %collective-permute-start = (bf16[8,4096]{1,0:T(8,128)(2,1)S(1)}, bf16[8,4096]{1,0:T(8,128)(2,1)S(1)}, u32[]{:S(2)}, u32[]{:S(2)}) collective-permute-start(bf16[8,4096]{1,0:T(8,128)(2,1)S(1)} %get-tuple-element.330), channel_id=1, source_target_pairs={{0,1},{1,2},{2,3},{3,4},{4,5},{5,6},{6,7},{7,8},{8,9},{9,10},{10,1... | collective-permute-start | bytes 196616 | tf_op jit(solution)/shard_map/while/body/eval_jaxpr/ppermute | solution.py:9
  125.1 6.4 %collective-permute-start = (bf16[8,4096]{1,0:T(8,128)(2,1)S(1)}, bf16[8,4096]{1,0:T(8,128)(2,1)S(1)}, u32[]{:S(2)}, u32[]{:S(2)}) collective-permute-start(bf16[8,4096]{1,0:T(8,128)(2,1)S(1)} %get-tuple-element.330), channel_id=1, source_target_pairs={{0,1},{1,2},{2,3},{3,4},{4,5},{5,6},{6,7},{7,8},{8,9},{9,10},{10,1... | collective-permute-start | bytes 196616 | tf_op jit(solution)/shard_map/while/body/eval_jaxpr/ppermute | solution.py:9
  132.1 6.8 %collective-permute-start = (bf16[8,4096]{1,0:T(8,128)(2,1)S(1)}, bf16[8,4096]{1,0:T(8,128)(2,1)S(1)}, u32[]{:S(2)}, u32[]{:S(2)}) collective-permute-start(bf16[8,4096]{1,0:T(8,128)(2,1)S(1)} %get-tuple-element.330), channel_id=1, source_target_pairs={{0,1},{1,2},{2,3},{3,4},{4,5},{5,6},{6,7},{7,8},{8,9},{9,10},{10,1... | collective-permute-start | bytes 196616 | tf_op jit(solution)/shard_map/while/body/eval_jaxpr/ppermute | solution.py:9
  139.5 6.4 %collective-permute-start = (bf16[8,4096]{1,0:T(8,128)(2,1)S(1)}, bf16[8,4096]{1,0:T(8,128)(2,1)S(1)}, u32[]{:S(2)}, u32[]{:S(2)}) collective-permute-start(bf16[8,4096]{1,0:T(8,128)(2,1)S(1)} %get-tuple-element.330), channel_id=1, source_target_pairs={{0,1},{1,2},{2,3},{3,4},{4,5},{5,6},{6,7},{7,8},{8,9},{9,10},{10,1... | collective-permute-start | bytes 196616 | tf_op jit(solution)/shard_map/while/body/eval_jaxpr/ppermute | solution.py:9
  146.6 6.4 %collective-permute-start = (bf16[8,4096]{1,0:T(8,128)(2,1)S(1)}, bf16[8,4096]{1,0:T(8,128)(2,1)S(1)}, u32[]{:S(2)}, u32[]{:S(2)}) collective-permute-start(bf16[8,4096]{1,0:T(8,128)(2,1)S(1)} %get-tuple-element.330), channel_id=1, source_target_pairs={{0,1},{1,2},{2,3},{3,4},{4,5},{5,6},{6,7},{7,8},{8,9},{9,10},{10,1... | collective-permute-start | bytes 196616 | tf_op jit(solution)/shard_map/while/body/eval_jaxpr/ppermute | solution.py:9
  153.6 6.4 %collective-permute-start = (bf16[8,4096]{1,0:T(8,128)(2,1)S(1)}, bf16[8,4096]{1,0:T(8,128)(2,1)S(1)}, u32[]{:S(2)}, u32[]{:S(2)}) collective-permute-start(bf16[8,4096]{1,0:T(8,128)(2,1)S(1)} %get-tuple-element.330), channel_id=1, source_target_pairs={{0,1},{1,2},{2,3},{3,4},{4,5},{5,6},{6,7},{7,8},{8,9},{9,10},{10,1... | collective-permute-start | bytes 196616 | tf_op jit(solution)/shard_map/while/body/eval_jaxpr/ppermute | solution.py:9
  160.7 6.4 %collective-permute-start = (bf16[8,4096]{1,0:T(8,128)(2,1)S(1)}, bf16[8,4096]{1,0:T(8,128)(2,1)S(1)}, u32[]{:S(2)}, u32[]{:S(2)}) collective-permute-start(bf16[8,4096]{1,0:T(8,128)(2,1)S(1)} %get-tuple-element.330), channel_id=1, source_target_pairs={{0,1},{1,2},{2,3},{3,4},{4,5},{5,6},{6,7},{7,8},{8,9},{9,10},{10,1... | collective-permute-start | bytes 196616 | tf_op jit(solution)/shard_map/while/body/eval_jaxpr/ppermute | solution.py:9
  167.7 6.4 %collective-permute-start = (bf16[8,4096]{1,0:T(8,128)(2,1)S(1)}, bf16[8,4096]{1,0:T(8,128)(2,1)S(1)}, u32[]{:S(2)}, u32[]{:S(2)}) collective-permute-start(bf16[8,4096]{1,0:T(8,128)(2,1)S(1)} %get-tuple-element.330), channel_id=1, source_target_pairs={{0,1},{1,2},{2,3},{3,4},{4,5},{5,6},{6,7},{7,8},{8,9},{9,10},{10,1... | collective-permute-start | bytes 196616 | tf_op jit(solution)/shard_map/while/body/eval_jaxpr/ppermute | solution.py:9
  174.8 6.4 %collective-permute-start = (bf16[8,4096]{1,0:T(8,128)(2,1)S(1)}, bf16[8,4096]{1,0:T(8,128)(2,1)S(1)}, u32[]{:S(2)}, u32[]{:S(2)}) collective-permute-start(bf16[8,4096]{1,0:T(8,128)(2,1)S(1)} %get-tuple-element.330), channel_id=1, source_target_pairs={{0,1},{1,2},{2,3},{3,4},{4,5},{5,6},{6,7},{7,8},{8,9},{9,10},{10,1... | collective-permute-start | bytes 196616 | tf_op jit(solution)/shard_map/while/body/eval_jaxpr/ppermute | solution.py:9
  181.8 6.4 %collective-permute-start = (bf16[8,4096]{1,0:T(8,128)(2,1)S(1)}, bf16[8,4096]{1,0:T(8,128)(2,1)S(1)}, u32[]{:S(2)}, u32[]{:S(2)}) collective-permute-start(bf16[8,4096]{1,0:T(8,128)(2,1)S(1)} %get-tuple-element.330), channel_id=1, source_target_pairs={{0,1},{1,2},{2,3},{3,4},{4,5},{5,6},{6,7},{7,8},{8,9},{9,10},{10,1... | collective-permute-start | bytes 196616 | tf_op jit(solution)/shard_map/while/body/eval_jaxpr/ppermute | solution.py:9
Sparse Core Ops, SparseCore 0:
  79.4 62.7 reduce-scatter.1
where the time goes:
time: 257 us; the launch traced here: 255 us
  waiting for transfers between devices  97 us (38%)
  blocking collectives  57.7 us (22%)
  other arithmetic  40.9 us (16%)
  matrix products  22.7 us (9%)
  local copies, waits for them, and re-layouts  21.7 us (8%)
  between operations  14.8 us (6%)
    ppermute x15, waiting for transfers between devices, passed_along(): lax.ppermute(value, axis, [(i, (i + by) % devices) for i in range(devices)])  97 us
    unnamed x1, blocking collectives  57.7 us
    scatter-add x4, other arithmetic, add_group(): return (totals.at[:, group_cols, :].add(products), None)  40.8 us
    gather x4, local copies, waits for them, and re-layouts, add_group(): selected = jnp.take(tiled, group_rows, axis=1)  11.7 us
    dot_general x4, matrix products, add_group(): jnp.einsum('ejb,jbc->ejc', selected, weights, preferred_element_type=jnp....  11.3 us
    dot_general x16, matrix products, tile_for_queries(): lax.dot_general(inv_gram, query_block, contract, preferred_element_type=j...  10.3 us
  transfers between devices with their start and end apart: 16, of which 15 were waited for; matrix products, arithmetic and copies ran while one was open for 4% of the time, Pallas kernels for 0%

commit v1 on v0

--- a/solution.py
+++ b/solution.py
@@ -1,7 +1,14 @@
+import functools
+
 import jax
 import jax.numpy as jnp
 from jax import lax
+from jax.experimental import pallas as pl
+from jax.experimental.pallas import tpu as pltpu
 from jax.sharding import PartitionSpec as P
+
+MESH = pl.DeviceIdType.MESH
+V_PIECES = 8
 
 
 def passed_along(value, axis, by):
@@ -75,6 +82,260 @@
     )
 
 
+def remote(src, dst, send_sem, recv_sem, device):
+    return pltpu.make_async_remote_copy(
+        src_ref=src,
+        dst_ref=dst,
+        send_sem=send_sem,
+        recv_sem=recv_sem,
+        device_id={"blk": device},
+        device_id_type=MESH,
+    )
+
+
+def fused_kernel(
+    n, table, grads, values_hbm, gram_hbm, queries, out,
+    values, gram, all_queries, pair_out, pair_in, far_out, far_in, score_out, score_in,
+    values_sem, gram_sem, query_send, query_recv, pass_send, pair_send, pair_recv,
+    far_send, far_recv, score_send, score_recv,
+):
+    chips = n // 2
+    me = lax.axis_index("blk")
+    chip = me // 2
+    core = me % 2
+    sibling = 2 * chip + 1 - core
+    examples, params = grads.shape
+    slots, side = values_hbm.shape[0], values_hbm.shape[1]
+    width, feature_dim = gram.shape
+    wide = width // side
+    col_blocks = feature_dim // side
+    row_blocks = params // side
+    half = feature_dim // 2
+    query_rows = queries.shape[0]
+    out_rows = out.shape[0]
+    piece = slots // V_PIECES
+
+    barrier = pltpu.get_barrier_semaphore()
+
+    def greet(k, _):
+        pl.semaphore_signal(barrier, inc=1, device_id={"blk": (me + k) % n}, device_id_type=MESH)
+        return 0
+
+    lax.fori_loop(1, n, greet, 0)
+
+    def values_copy(i):
+        part = pl.ds(i * piece, piece)
+        return pltpu.make_async_copy(values_hbm.at[part], values.at[part], values_sem.at[i])
+
+    for i in range(V_PIECES):
+        values_copy(i).start()
+    gram_copy = pltpu.make_async_copy(gram_hbm, gram, gram_sem)
+    gram_copy.start()
+
+    own_queries = queries[...].astype(jnp.float32)
+    all_queries[me] = jnp.concatenate(
+        [own_queries[:, :half], own_queries[:, half:]], axis=0
+    ).astype(jnp.bfloat16)
+    values[slots] = jnp.zeros((side, side), jnp.bfloat16)
+    pl.semaphore_wait(barrier, n - 1)
+
+    def query_copy(k, to, which, sems):
+        return remote(all_queries.at[which], all_queries.at[which], sems.at[k], query_recv.at[which], to)
+
+    query_copy(0, sibling, me, query_send).start()
+
+    def send_queries(k, _):
+        query_copy(k, 2 * ((chip + k) % chips) + core, me, query_send).start()
+        return 0
+
+    lax.fori_loop(1, chips, send_queries, 0)
+
+    for i in range(V_PIECES):
+        values_copy(i).wait()
+
+    def partial(owner):
+        total = jnp.zeros((examples, width), jnp.float32)
+        for r in range(0, row_blocks, 2):
+            tile = jnp.concatenate(
+                [
+                    jnp.concatenate(
+                        [values[table[(r + i) * col_blocks + owner * wide + j]] for j in range(wide)], axis=1
+                    )
+                    for i in range(2)
+                ],
+                axis=0,
+            )
+            total += jnp.dot(
+                grads[:, r * side : (r + 2) * side], tile, preferred_element_type=jnp.float32
+            )
+        return total
+
+    def pair_copy(k):
+        return remote(pair_out.at[k], pair_in.at[k], pair_send.at[k], pair_recv.at[k], sibling)
+
+    def for_sibling(k, _):
+        owner = 2 * ((chip + 1 + k) % chips) + 1 - core
+        pair_out[k] = partial(owner)
+        pair_copy(k).start()
+        return 0
+
+    lax.fori_loop(0, chips, for_sibling, 0)
+
+    def far_copy(k):
+        to = 2 * ((chip + 1 + k) % chips) + core
+        return remote(far_out.at[k], far_in.at[k], far_send.at[k], far_recv.at[k], to)
+
+    def for_far(k, _):
+        total = partial(2 * ((chip + 1 + k) % chips) + core)
+        pair_copy(k).wait_recv()
+        far_out[k] = (total + pair_in[k]).astype(jnp.bfloat16)
+        far_copy(k).start()
+        return 0
+
+    lax.fori_loop(0, chips - 1, for_far, 0)
+    features = partial(me)
+    pair_copy(chips - 1).wait_recv()
+    features += pair_in[chips - 1]
+
+    def pass_queries(k, _):
+        which = 2 * ((chip + chips - k) % chips) + core
+        query_copy(k, sibling, which, pass_send).wait_recv()
+        query_copy(k, sibling, which, pass_send).start()
+        return 0
+
+    lax.fori_loop(1, chips, pass_queries, 0)
+
+    def wait_passed(k, _):
+        which = 2 * ((chip + chips - k) % chips) + 1 - core
+        query_copy(k, sibling, which, pass_send).wait_recv()
+        return 0
+
+    lax.fori_loop(0, chips, wait_passed, 0)
+    gram_copy.wait()
+
+    stacked = all_queries[...].reshape(n * 2 * query_rows, half)
+    contract = (((1,), (1,)), ((), ()))
+    first = lax.dot_general(gram[:, :half], stacked, contract, preferred_element_type=jnp.float32)
+    second = lax.dot_general(gram[:, half:], stacked, contract, preferred_element_type=jnp.float32)
+    columns = n * 2 * query_rows
+    whitened = (first + pltpu.roll(second, columns - query_rows, 1)).astype(jnp.bfloat16)
+    row = lax.broadcasted_iota(jnp.int32, (columns, n * query_rows), 0)
+    col = lax.broadcasted_iota(jnp.int32, (columns, n * query_rows), 1)
+    pick = (row == (col // query_rows) * (2 * query_rows) + col % query_rows).astype(jnp.bfloat16)
+    whitened = jnp.dot(whitened, pick, preferred_element_type=jnp.float32).astype(jnp.bfloat16)
+
+    for k in range(chips - 1):
+        far_copy(k).wait_recv()
+        features += far_in[k].astype(jnp.float32)
+    high = features.astype(jnp.bfloat16)
+    rest = features - high.astype(jnp.float32)
+    middle = rest.astype(jnp.bfloat16)
+    low = (rest - middle.astype(jnp.float32)).astype(jnp.bfloat16)
+    scores = jnp.dot(high, whitened, preferred_element_type=jnp.float32)
+    scores += jnp.dot(middle, whitened, preferred_element_type=jnp.float32)
+    scores += jnp.dot(low, whitened, preferred_element_type=jnp.float32)
+    for d in range(n):
+        score_out[d, :out_rows, :] = scores[d * out_rows : (d + 1) * out_rows]
+
+    def score_copy(k):
+        to = (me + k) % n
+        return remote(score_out.at[to], score_in.at[k], score_send.at[k], score_recv.at[k], to)
+
+    def send_scores(k, _):
+        score_copy(k).start()
+        return 0
+
+    lax.fori_loop(1, n, send_scores, 0)
+    result = score_out[me]
+    for k in range(1, n):
+        score_copy(k).wait_recv()
+        result += score_in[k]
+    out[...] = result[:out_rows]
+
+    def drain(k, _):
+        query_copy(k, sibling, me, query_send).wait_send()
+        pair_copy(k).wait_send()
+        return 0
+
+    lax.fori_loop(0, chips, drain, 0)
+
+    def drain_far(k, _):
+        far_copy(k).wait_send()
+        query_copy(k + 1, sibling, me, pass_send).wait_send()
+        return 0
+
+    lax.fori_loop(0, chips - 1, drain_far, 0)
+
+    def drain_scores(k, _):
+        score_copy(k).wait_send()
+        return 0
+
+    lax.fori_loop(1, n, drain_scores, 0)
+
+
+def fused_shards(grads, block_values, block_rows, block_cols, block_counts, inv_gram, queries):
+    n = lax.axis_size("blk")
+    chips = n // 2
+    examples, params = grads.shape
+    slots, side = block_values.shape[0], block_values.shape[1]
+    width, feature_dim = inv_gram.shape
+    query_rows = queries.shape[0]
+    out_rows = examples // n
+    padded_rows = -(-out_rows // 8) * 8
+    places = (params // side) * (feature_dim // side)
+    slot_ids = jnp.arange(slots, dtype=jnp.int32)
+    place = jnp.where(slot_ids < block_counts[0], block_rows * (feature_dim // side) + block_cols, -1)
+    hit = place[None, :] == jnp.arange(places, dtype=jnp.int32)[:, None]
+    table = jnp.sum(jnp.where(hit, slot_ids[None, :] - slots, 0), axis=1) + slots
+    vmem = pl.BlockSpec(memory_space=pltpu.VMEM)
+    anywhere = pl.BlockSpec(memory_space=pl.ANY)
+    dma = pltpu.SemaphoreType.DMA
+    return pl.pallas_call(
+        functools.partial(fused_kernel, n),
+        out_shape=jax.ShapeDtypeStruct((out_rows, n * query_rows), jnp.float32),
+        in_specs=[pl.BlockSpec(memory_space=pltpu.SMEM), vmem, anywhere, anywhere, vmem],
+        out_specs=vmem,
+        scratch_shapes=[
+            pltpu.VMEM((slots + 1, side, side), jnp.bfloat16),
+            pltpu.VMEM((width, feature_dim), jnp.bfloat16),
+            pltpu.VMEM((n, 2 * query_rows, feature_dim // 2), jnp.bfloat16),
+            pltpu.VMEM((chips, examples, width), jnp.float32),
+            pltpu.VMEM((chips, examples, width), jnp.float32),
+            pltpu.VMEM((chips, examples, width), jnp.bfloat16),
+            pltpu.VMEM((chips, examples, width), jnp.bfloat16),
+            pltpu.VMEM((n, padded_rows, n * query_rows), jnp.float32),
+            pltpu.VMEM((n, padded_rows, n * query_rows), jnp.float32),
+            dma((V_PIECES,)),
+            dma(()),
+            dma((chips,)),
+            dma((n,)),
+            dma((chips,)),
+            dma((chips,)),
+            dma((chips,)),
+            dma((chips,)),
+            dma((chips,)),
+            dma((n,)),
+            dma((n,)),
+        ],
+        compiler_params=pltpu.CompilerParams(
+            collective_id=0, has_side_effects=True, vmem_limit_bytes=48 * 1024 * 1024
+        ),
+    )(table, grads, block_values, inv_gram, queries)
+
+
+def fits(mesh, args):
+    grads, block_values, _, _, _, inv_gram, queries = args
+    n, groups = mesh.shape["blk"], mesh.shape["groups"]
+    side = block_values.shape[1]
+    width = inv_gram.shape[0] // n
+    return (
+        n % 2 == 0
+        and width % side == 0
+        and grads.shape[0] // groups % 16 == 0
+        and queries.shape[0] // (groups * n) == 8
+    )
+
+
 def solution(mesh):
     placed = (
         P("groups", "blk"),
@@ -85,6 +346,11 @@
         P("blk", None),
         P(("groups", "blk"), None),
     )
-    return jax.shard_map(
-        shards, mesh=mesh, in_specs=placed, out_specs=P(("groups", "blk"), None), check_vma=False
-    )
+
+    def whole(*args):
+        body = fused_shards if fits(mesh, args) else shards
+        return jax.shard_map(
+            body, mesh=mesh, in_specs=placed, out_specs=P(("groups", "blk"), None), check_vma=False
+        )(*args)
+
+    return whole

time: 257 us -> 40.4 us (0.16)
  waiting for transfers between devices: 97 us -> 0 us
  blocking collectives: 57.7 us -> 0 us
  other arithmetic: 40.9 us -> 0.86 us
  Pallas kernels: 0 us -> 34.6 us
  matrix products: 22.7 us -> 0 us
  local copies, waits for them, and re-layouts: 21.7 us -> 4.02 us
  between operations: 14.8 us -> 0.68 us
    ppermute x15 -> x0, waiting for transfers between devices: 97 us -> none  [passed_along(): lax.ppermute(value, axis, [(i, (i + by) % devices) for i in range(devices)])]
    unnamed x1 -> x0, blocking collectives: 57.7 us -> none
    scatter-add x4 -> x0, other arithmetic: 40.8 us -> none  [add_group(): return (totals.at[:, group_cols, :].add(products), None)]
    pallas_call x0 -> x1, Pallas kernels: none -> 34.6 us  [fused_shards(): pl.pallas_call(functools.partial(fused_kernel, n), out_shape=jax.ShapeDty...]
    dot_general x21 -> x0, matrix products: 22.7 us -> none  [the longest x4 11.3 us: add_group(): jnp.einsum('ejb,jbc->ejc', selected, weights, preferred_element_type=jnp....]
    gather x4 -> x0, local copies, waits for them, and re-layouts: 11.7 us -> none  [add_group(): selected = jnp.take(tiled, group_rows, axis=1)]
    reshape x3 -> x0, local copies, waits for them, and re-layouts: 4.38 us -> none  [the longest x1 2.86 us: shards(): partial_features = totals.reshape(examples, feature_dim)]
  transfers between devices with their start and end apart: 16 -> 0, of which waited for: 15 -> 0; matrix products, arithmetic and copies ran while one was open for 4% -> 0% of each run, Pallas kernels for 0% -> 0%
where the time goes in v1:
time: 40.4 us; the launch traced here: 40.1 us
  Pallas kernels  34.6 us (86%)
  local copies, waits for them, and re-layouts  4.02 us (10%)
  other arithmetic  0.86 us (2%)
  between operations  0.68 us (2%)
    pallas_call x1, Pallas kernels, fused_shards(): pl.pallas_call(functools.partial(fused_kernel, n), out_shape=jax.ShapeDty...  34.6 us
    unnamed x7, local copies, waits for them, and re-layouts  4.02 us

profile of v1, /device:TPU:0, one launch (start us, length us, event | category | flops | bytes accessed | tf_op | source)
XLA Modules:
  0.0 40.1 jit_solution(8799563276747060275)
XLA Ops:
  0.7 0.7 %compare_select_fusion = (s32[256]{0:T(256)S(1)}, s32[256]{0:T(256)S(1)}) fusion(s32[256]{0:T(256)} %param.10, s32[256]{0:T(256)} %param.9, s32[]{:T(128)} %bitcast.1), kind=kLoop, calls=%fused_computation.2 | loop fusion | flops 1280 | bytes 4100 | tf_op jit(solution)/shard_map/jit(_where)/select_n | solution.py:287
  1.4 0.1 select_reduce_fusion
  1.5 0.0 copy-start
  1.5 1.6 %copy-done = bf16[256,4096]{1,0:T(8,128)(2,1)S(1)} copy-done((bf16[256,4096]{1,0:T(8,128)(2,1)S(1)}, bf16[256,4096]{1,0:T(8,128)(2,1)}, u32[]{:S(2)}) %copy-start) | copy-done | bytes 2097176
  3.1 0.0 copy-start.1
  3.1 1.0 %copy-done.1 = bf16[96,2048]{1,0:T(8,128)(2,1)S(1)} copy-done((bf16[96,2048]{1,0:T(8,128)(2,1)S(1)}, bf16[96,2048]{1,0:T(8,128)(2,1)}, u32[]{:S(2)}) %copy-start.1) | copy-done | bytes 393240
  4.1 0.0 copy-start.2
  4.1 0.8 %copy-done.2 = bf16[8,4096]{1,0:T(8,128)(2,1)S(1)} copy-done((bf16[8,4096]{1,0:T(8,128)(2,1)S(1)}, bf16[8,4096]{1,0:T(8,128)(2,1)}, u32[]{:S(2)}) %copy-start.2) | copy-done | bytes 65560
  4.9 34.6 %shard_map.73 = f32[6,128]{1,0:T(8,128)S(1)} custom-call(s32[512]{0:T(512)S(1)} %broadcast_add_fusion.table, bf16[96,2048]{1,0:T(8,128)(2,1)S(1)} %copy-done.1, bf16[256,128,128]{2,1,0:T(8,128)(2,1)} %values_hbm.1, bf16[256,4096]{1,0:T(8,128)(2,1)S(1)} %copy-done, bf16[8,4096]{1,0:T(8,128)(2,1)S(1)} %copy-done.2), custom_call_target="tpu_custom_call" | custom-call | tf_op jit(solution)/shard_map/pallas_call | solution.py:293
  39.5 0.6 %copy.10 = f32[6,128]{1,0:T(8,128)} copy(f32[6,128]{1,0:T(8,128)S(1)} %shard_map.73) | data formatting | bytes 6144
  (1 shorter events, 0.0 us)
Async XLA Ops:
  1.5 1.6 %copy-start = (bf16[256,4096]{1,0:T(8,128)(2,1)S(1)}, bf16[256,4096]{1,0:T(8,128)(2,1)}, u32[]{:S(2)}) copy-start(bf16[256,4096]{1,0:T(8,128)(2,1)} %gram_hbm.1) | copy-start | bytes 6291460
  3.1 1.0 %copy-start.1 = (bf16[96,2048]{1,0:T(8,128)(2,1)S(1)}, bf16[96,2048]{1,0:T(8,128)(2,1)}, u32[]{:S(2)}) copy-start(bf16[96,2048]{1,0:T(8,128)(2,1)} %grads.1) | copy-start | bytes 1179652
  4.1 0.8 %copy-start.2 = (bf16[8,4096]{1,0:T(8,128)(2,1)S(1)}, bf16[8,4096]{1,0:T(8,128)(2,1)}, u32[]{:S(2)}) copy-start(bf16[8,4096]{1,0:T(8,128)(2,1)} %queries.1) | copy-start | bytes 196612

commit v2 on v1

--- a/solution.py
+++ b/solution.py
@@ -94,16 +94,21 @@
 
 
 def fused_kernel(
-    n, table, grads, values_hbm, gram_hbm, queries, out,
-    values, gram, all_queries, pair_out, pair_in, far_out, far_in, score_out, score_in,
-    values_sem, gram_sem, query_send, query_recv, pass_send, pair_send, pair_recv,
-    far_send, far_recv, score_send, score_recv,
+    n, rows_hbm, cols_hbm, counts, grads_hbm, values_hbm, gram_hbm, queries, out,
+    rows, cols, table_rows, table, grads, values, gram, all_queries, pair_out, pair_in,
+    near_out, near_in, far_out, far_in, score_out, score_in,
+    slot_sems, values_sem, load_sems, query_send, query_recv, pass_near, pass_far, pass_pair,
+    pair_send, pair_recv, near_send, near_recv, far_send, far_recv, score_send, score_recv,
 ):
-    chips = n // 2
+    depth = n // 4
     me = lax.axis_index("blk")
-    chip = me // 2
-    core = me % 2
-    sibling = 2 * chip + 1 - core
+    z, y, core = me // 4, (me // 2) % 2, me % 2
+
+    def device(at_z, at_y, at_core):
+        return 4 * at_z + 2 * at_y + at_core
+
+    sibling = device(z, y, 1 - core)
+    across = device(z, 1 - y, core)
     examples, params = grads.shape
     slots, side = values_hbm.shape[0], values_hbm.shape[1]
     width, feature_dim = gram.shape
@@ -114,6 +119,7 @@
     query_rows = queries.shape[0]
     out_rows = out.shape[0]
     piece = slots // V_PIECES
+    lanes = rows.shape[1]
 
     barrier = pltpu.get_barrier_semaphore()
 
@@ -122,14 +128,21 @@
         return 0
 
     lax.fori_loop(1, n, greet, 0)
+
+    rows_copy = pltpu.make_async_copy(rows_hbm, rows, slot_sems.at[0])
+    cols_copy = pltpu.make_async_copy(cols_hbm, cols, slot_sems.at[1])
+    rows_copy.start()
+    cols_copy.start()
 
     def values_copy(i):
         part = pl.ds(i * piece, piece)
         return pltpu.make_async_copy(values_hbm.at[part], values.at[part], values_sem.at[i])
 
+    grads_copy = pltpu.make_async_copy(grads_hbm, grads, load_sems.at[0])
+    gram_copy = pltpu.make_async_copy(gram_hbm, gram, load_sems.at[1])
+    grads_copy.start()
     for i in range(V_PIECES):
         values_copy(i).start()
-    gram_copy = pltpu.make_async_copy(gram_hbm, gram, gram_sem)
     gram_copy.start()
 
     own_queries = queries[...].astype(jnp.float32)
@@ -139,28 +152,50 @@
     values[slots] = jnp.zeros((side, side), jnp.bfloat16)
     pl.semaphore_wait(barrier, n - 1)
 
-    def query_copy(k, to, which, sems):
-        return remote(all_queries.at[which], all_queries.at[which], sems.at[k], query_recv.at[which], to)
-
-    query_copy(0, sibling, me, query_send).start()
+    def query_copy(which, to, send_sem):
+        return remote(all_queries.at[which], all_queries.at[which], send_sem, query_recv.at[which], to)
 
     def send_queries(k, _):
-        query_copy(k, 2 * ((chip + k) % chips) + core, me, query_send).start()
-        return 0
-
-    lax.fori_loop(1, chips, send_queries, 0)
-
+        query_copy(me, device((z + k) % depth, y, core), query_send.at[k]).start()
+        return 0
+
+    lax.fori_loop(1, depth, send_queries, 0)
+    query_copy(me, across, query_send.at[depth]).start()
+    query_copy(me, sibling, query_send.at[0]).start()
+
+    rows_copy.wait()
+    cols_copy.wait()
+    place = rows[...] * col_blocks + cols[...]
+    slot_at = lax.broadcasted_iota(jnp.int32, (lanes, lanes), 0)
+    lane_at = lax.broadcasted_iota(jnp.int32, (lanes, lanes), 1)
+    columns = [
+        jnp.transpose(jnp.broadcast_to(place[s : s + 1], (lanes, lanes)))
+        for s in range(slots // lanes)
+    ]
+    for t in range(table.shape[0]):
+        found = jnp.full((1, lanes), slots, jnp.int32)
+        for s, column in enumerate(columns):
+            slot = slot_at + s * lanes
+            hit = (column == lane_at + t * lanes) & (slot < counts[0])
+            found += jnp.sum(jnp.where(hit, slot - slots, 0), axis=0, keepdims=True)
+        table_rows[t : t + 1] = found
+    table_copy = pltpu.make_async_copy(table_rows, table, load_sems.at[2])
+    table_copy.start()
+    table_copy.wait()
+    grads_copy.wait()
     for i in range(V_PIECES):
         values_copy(i).wait()
+
+    def block(row_block, col_block):
+        at = row_block * col_blocks + col_block
+        return values[table[at // lanes, at % lanes]]
 
     def partial(owner):
         total = jnp.zeros((examples, width), jnp.float32)
         for r in range(0, row_blocks, 2):
             tile = jnp.concatenate(
                 [
-                    jnp.concatenate(
-                        [values[table[(r + i) * col_blocks + owner * wide + j]] for j in range(wide)], axis=1
-                    )
+                    jnp.concatenate([block(r + i, owner * wide + j) for j in range(wide)], axis=1)
                     for i in range(2)
                 ],
                 axis=0,
@@ -173,58 +208,80 @@
     def pair_copy(k):
         return remote(pair_out.at[k], pair_in.at[k], pair_send.at[k], pair_recv.at[k], sibling)
 
+    def near_copy(k):
+        return remote(near_out.at[k], near_in.at[k], near_send.at[k], near_recv.at[k], across)
+
+    def far_copy(k):
+        to = device((z + 1 + k) % depth, y, core)
+        return remote(far_out.at[k], far_in.at[k], far_send.at[k], far_recv.at[k], to)
+
     def for_sibling(k, _):
-        owner = 2 * ((chip + 1 + k) % chips) + 1 - core
-        pair_out[k] = partial(owner)
+        pair_out[k] = partial(device((z + 1 + k) % depth, (y + 1 + k // depth) % 2, 1 - core))
         pair_copy(k).start()
         return 0
 
-    lax.fori_loop(0, chips, for_sibling, 0)
-
-    def far_copy(k):
-        to = 2 * ((chip + 1 + k) % chips) + core
-        return remote(far_out.at[k], far_in.at[k], far_send.at[k], far_recv.at[k], to)
-
-    def for_far(k, _):
-        total = partial(2 * ((chip + 1 + k) % chips) + core)
+    def pass_one(k):
+        which = device((z + depth - k) % depth, y, core)
+        query_copy(which, across, pass_near.at[k]).wait_recv()
+        query_copy(which, across, pass_near.at[k]).start()
+        query_copy(which, sibling, pass_far.at[k]).start()
+
+    lax.fori_loop(0, 2 * depth, for_sibling, 0)
+    pass_one(1)
+
+    def for_near(k, _):
+        total = partial(device((z + 1 + k) % depth, 1 - y, core))
         pair_copy(k).wait_recv()
-        far_out[k] = (total + pair_in[k]).astype(jnp.bfloat16)
+        near_out[k] = (total + pair_in[k]).astype(jnp.bfloat16)
+        near_copy(k).start()
+        return 0
+
+    lax.fori_loop(0, depth, for_near, 0)
+    for k in range(2, depth - 1):
+        pass_one(k)
+
+    def for_far(k):
+        total = partial(device((z + 1 + k) % depth, y, core))
+        pair_copy(depth + k).wait_recv()
+        near_copy(k).wait_recv()
+        return total + pair_in[depth + k] + near_in[k].astype(jnp.float32)
+
+    def send_far(k, _):
+        far_out[k] = for_far(k).astype(jnp.bfloat16)
         far_copy(k).start()
         return 0
 
-    lax.fori_loop(0, chips - 1, for_far, 0)
-    features = partial(me)
-    pair_copy(chips - 1).wait_recv()
-    features += pair_in[chips - 1]
-
-    def pass_queries(k, _):
-        which = 2 * ((chip + chips - k) % chips) + core
-        query_copy(k, sibling, which, pass_send).wait_recv()
-        query_copy(k, sibling, which, pass_send).start()
-        return 0
-
-    lax.fori_loop(1, chips, pass_queries, 0)
+    lax.fori_loop(0, depth - 1, send_far, 0)
+    pass_one(depth - 1)
+    features = for_far(depth - 1)
+
+    def pass_across(k, _):
+        which = device((z + depth - k) % depth, 1 - y, core)
+        query_copy(which, sibling, pass_pair.at[k]).wait_recv()
+        query_copy(which, sibling, pass_pair.at[k]).start()
+        return 0
+
+    lax.fori_loop(0, depth, pass_across, 0)
 
     def wait_passed(k, _):
-        which = 2 * ((chip + chips - k) % chips) + 1 - core
-        query_copy(k, sibling, which, pass_send).wait_recv()
-        return 0
-
-    lax.fori_loop(0, chips, wait_passed, 0)
+        query_copy(2 * k + 1 - core, sibling, query_send.at[0]).wait_recv()
+        return 0
+
+    lax.fori_loop(0, 2 * depth, wait_passed, 0)
     gram_copy.wait()
 
     stacked = all_queries[...].reshape(n * 2 * query_rows, half)
     contract = (((1,), (1,)), ((), ()))
     first = lax.dot_general(gram[:, :half], stacked, contract, preferred_element_type=jnp.float32)
     second = lax.dot_general(gram[:, half:], stacked, contract, preferred_element_type=jnp.float32)
-    columns = n * 2 * query_rows
-    whitened = (first + pltpu.roll(second, columns - query_rows, 1)).astype(jnp.bfloat16)
-    row = lax.broadcasted_iota(jnp.int32, (columns, n * query_rows), 0)
-    col = lax.broadcasted_iota(jnp.int32, (columns, n * query_rows), 1)
+    across_all = n * 2 * query_rows
+    whitened = (first + pltpu.roll(second, across_all - query_rows, 1)).astype(jnp.bfloat16)
+    row = lax.broadcasted_iota(jnp.int32, (across_all, n * query_rows), 0)
+    col = lax.broadcasted_iota(jnp.int32, (across_all, n * query_rows), 1)
     pick = (row == (col // query_rows) * (2 * query_rows) + col % query_rows).astype(jnp.bfloat16)
     whitened = jnp.dot(whitened, pick, preferred_element_type=jnp.float32).astype(jnp.bfloat16)
 
-    for k in range(chips - 1):
+    for k in range(depth - 1):
         far_copy(k).wait_recv()
         features += far_in[k].astype(jnp.float32)
     high = features.astype(jnp.bfloat16)
@@ -252,19 +309,28 @@
         result += score_in[k]
     out[...] = result[:out_rows]
 
-    def drain(k, _):
-        query_copy(k, sibling, me, query_send).wait_send()
+    def drain_pair(k, _):
         pair_copy(k).wait_send()
         return 0
 
-    lax.fori_loop(0, chips, drain, 0)
+    lax.fori_loop(0, 2 * depth, drain_pair, 0)
+
+    def drain_depth(k, _):
+        near_copy(k).wait_send()
+        query_copy(me, sibling, query_send.at[k]).wait_send()
+        query_copy(me, sibling, pass_pair.at[k]).wait_send()
+        return 0
+
+    lax.fori_loop(0, depth, drain_depth, 0)
+    query_copy(me, sibling, query_send.at[depth]).wait_send()
 
     def drain_far(k, _):
         far_copy(k).wait_send()
-        query_copy(k + 1, sibling, me, pass_send).wait_send()
-        return 0
-
-    lax.fori_loop(0, chips - 1, drain_far, 0)
+        query_copy(me, sibling, pass_near.at[k + 1]).wait_send()
+        query_copy(me, sibling, pass_far.at[k + 1]).wait_send()
+        return 0
+
+    lax.fori_loop(0, depth - 1, drain_far, 0)
 
     def drain_scores(k, _):
         score_copy(k).wait_send()
@@ -275,7 +341,7 @@
 
 def fused_shards(grads, block_values, block_rows, block_cols, block_counts, inv_gram, queries):
     n = lax.axis_size("blk")
-    chips = n // 2
+    depth = n // 4
     examples, params = grads.shape
     slots, side = block_values.shape[0], block_values.shape[1]
     width, feature_dim = inv_gram.shape
@@ -283,44 +349,62 @@
     out_rows = examples // n
     padded_rows = -(-out_rows // 8) * 8
     places = (params // side) * (feature_dim // side)
-    slot_ids = jnp.arange(slots, dtype=jnp.int32)
-    place = jnp.where(slot_ids < block_counts[0], block_rows * (feature_dim // side) + block_cols, -1)
-    hit = place[None, :] == jnp.arange(places, dtype=jnp.int32)[:, None]
-    table = jnp.sum(jnp.where(hit, slot_ids[None, :] - slots, 0), axis=1) + slots
+    lanes = 128
     vmem = pl.BlockSpec(memory_space=pltpu.VMEM)
-    anywhere = pl.BlockSpec(memory_space=pl.ANY)
+    smem = pl.BlockSpec(memory_space=pltpu.SMEM)
+    hbm = pl.BlockSpec(memory_space=pltpu.HBM)
     dma = pltpu.SemaphoreType.DMA
     return pl.pallas_call(
         functools.partial(fused_kernel, n),
         out_shape=jax.ShapeDtypeStruct((out_rows, n * query_rows), jnp.float32),
-        in_specs=[pl.BlockSpec(memory_space=pltpu.SMEM), vmem, anywhere, anywhere, vmem],
+        in_specs=[hbm, hbm, smem, hbm, hbm, hbm, vmem],
         out_specs=vmem,
         scratch_shapes=[
+            pltpu.VMEM((slots // lanes, lanes), jnp.int32),
+            pltpu.VMEM((slots // lanes, lanes), jnp.int32),
+            pltpu.VMEM((places // lanes, lanes), jnp.int32),
+            pltpu.SMEM((places // lanes, lanes), jnp.int32),
+            pltpu.VMEM((examples, params), jnp.bfloat16),
             pltpu.VMEM((slots + 1, side, side), jnp.bfloat16),
             pltpu.VMEM((width, feature_dim), jnp.bfloat16),
             pltpu.VMEM((n, 2 * query_rows, feature_dim // 2), jnp.bfloat16),
-            pltpu.VMEM((chips, examples, width), jnp.float32),
-            pltpu.VMEM((chips, examples, width), jnp.float32),
-            pltpu.VMEM((chips, examples, width), jnp.bfloat16),
-            pltpu.VMEM((chips, examples, width), jnp.bfloat16),
+            pltpu.VMEM((2 * depth, examples, width), jnp.float32),
+            pltpu.VMEM((2 * depth, examples, width), jnp.float32),
+            pltpu.VMEM((depth, examples, width), jnp.bfloat16),
+            pltpu.VMEM((depth, examples, width), jnp.bfloat16),
+            pltpu.VMEM((depth, examples, width), jnp.bfloat16),
+            pltpu.VMEM((depth, examples, width), jnp.bfloat16),
             pltpu.VMEM((n, padded_rows, n * query_rows), jnp.float32),
             pltpu.VMEM((n, padded_rows, n * query_rows), jnp.float32),
+            dma((2,)),
             dma((V_PIECES,)),
-            dma(()),
-            dma((chips,)),
+            dma((3,)),
+            dma((depth + 1,)),
             dma((n,)),
-            dma((chips,)),
-            dma((chips,)),
-            dma((chips,)),
-            dma((chips,)),
-            dma((chips,)),
+            dma((depth,)),
+            dma((depth,)),
+            dma((depth,)),
+            dma((2 * depth,)),
+            dma((2 * depth,)),
+            dma((depth,)),
+            dma((depth,)),
+            dma((depth,)),
+            dma((depth,)),
             dma((n,)),
             dma((n,)),
         ],
         compiler_params=pltpu.CompilerParams(
-            collective_id=0, has_side_effects=True, vmem_limit_bytes=48 * 1024 * 1024
+            collective_id=0, has_side_effects=True, vmem_limit_bytes=63 * 1024 * 1024
         ),
-    )(table, grads, block_values, inv_gram, queries)
+    )(
+        block_rows.reshape(slots // lanes, lanes),
+        block_cols.reshape(slots // lanes, lanes),
+        block_counts,
+        grads,
+        block_values,
+        inv_gram,
+        queries,
+    )
 
 
 def fits(mesh, args):
@@ -329,8 +413,12 @@
     side = block_values.shape[1]
     width = inv_gram.shape[0] // n
     return (
-        n % 2 == 0
+        n % 4 == 0
+        and n > 8
+        and side == 128
         and width % side == 0
+        and block_values.shape[0] // n % 128 == 0
+        and grads.shape[1] // n % (2 * side) == 0
         and grads.shape[0] // groups % 16 == 0
         and queries.shape[0] // (groups * n) == 8
     )

time: 40.4 us -> 32.1 us (0.79)
  Pallas kernels: 34.6 us -> 29.9 us
  local copies, waits for them, and re-layouts: 4.02 us -> 1.28 us
  other arithmetic: 0.86 us -> 0 us
    pallas_call x1, Pallas kernels: 34.6 us -> 29.9 us  [fused_shards(): pl.pallas_call(functools.partial(fused_kernel, n), out_shape=jax.ShapeDty...]
    unnamed x7 -> x1, local copies, waits for them, and re-layouts: 4.02 us -> 1.28 us
    select_n x1 -> x0, other arithmetic: 0.7 us -> none  [fused_shards(): jnp.where(slot_ids < block_counts[0], block_rows * (feature_dim // side)...]
where the time goes in v2:
time: 32.1 us; the launch traced here: 31.9 us
  Pallas kernels  29.9 us (93%)
  local copies, waits for them, and re-layouts  1.28 us (4%)
  between operations  0.66 us (2%)
    pallas_call x1, Pallas kernels, fused_shards(): pl.pallas_call(functools.partial(fused_kernel, n), out_shape=jax.ShapeDty...  29.9 us
    unnamed x1, local copies, waits for them, and re-layouts  1.28 us

profile of v2, /device:TPU:0, one launch (start us, length us, event | category | flops | bytes accessed | tf_op | source)
XLA Modules:
  0.0 31.9 jit_solution(7681703748061415844)
XLA Ops:
  0.7 29.9 %shard_map.73 = f32[6,128]{1,0:T(8,128)} custom-call(s32[2,128]{1,0:T(2,128)} %bitcast.2, s32[2,128]{1,0:T(2,128)} %bitcast.3, s32[1]{0:T(128)S(6)} %copy.9.counts, bf16[96,2048]{1,0:T(8,128)(2,1)} %grads_hbm.1, bf16[256,128,128]{2,1,0:T(8,128)(2,1)} %values_hbm.1, bf16[256,4096]{1,0:T(8,128)(2,1)} %gram_hbm.1, bf16[8,4096]{1,0:T(8,128)(2,1)} %queries.1), custom_call_target="tpu_custom_call" | custom-call | tf_op jit(solution)/shard_map/pallas_call | solution.py:357
  30.6 1.3 %copy.10 = f32[6,128]{1,0:T(8,128)} copy(f32[6,128]{1,0:T(8,128)} %shard_map.73) | data formatting | bytes 6144

commit v3 on v2

--- a/solution.py
+++ b/solution.py
@@ -123,11 +123,9 @@
 
     barrier = pltpu.get_barrier_semaphore()
 
-    def greet(k, _):
-        pl.semaphore_signal(barrier, inc=1, device_id={"blk": (me + k) % n}, device_id_type=MESH)
-        return 0
-
-    lax.fori_loop(1, n, greet, 0)
+    peers = [sibling, across] + [device((z + k) % depth, y, core) for k in range(1, depth)]
+    for peer in peers:
+        pl.semaphore_signal(barrier, inc=1, device_id={"blk": peer}, device_id_type=MESH)
 
     rows_copy = pltpu.make_async_copy(rows_hbm, rows, slot_sems.at[0])
     cols_copy = pltpu.make_async_copy(cols_hbm, cols, slot_sems.at[1])
@@ -150,19 +148,6 @@
         [own_queries[:, :half], own_queries[:, half:]], axis=0
     ).astype(jnp.bfloat16)
     values[slots] = jnp.zeros((side, side), jnp.bfloat16)
-    pl.semaphore_wait(barrier, n - 1)
-
-    def query_copy(which, to, send_sem):
-        return remote(all_queries.at[which], all_queries.at[which], send_sem, query_recv.at[which], to)
-
-    def send_queries(k, _):
-        query_copy(me, device((z + k) % depth, y, core), query_send.at[k]).start()
-        return 0
-
-    lax.fori_loop(1, depth, send_queries, 0)
-    query_copy(me, across, query_send.at[depth]).start()
-    query_copy(me, sibling, query_send.at[0]).start()
-
     rows_copy.wait()
     cols_copy.wait()
     place = rows[...] * col_blocks + cols[...]
@@ -181,6 +166,20 @@
         table_rows[t : t + 1] = found
     table_copy = pltpu.make_async_copy(table_rows, table, load_sems.at[2])
     table_copy.start()
+
+    pl.semaphore_wait(barrier, len(peers))
+
+    def query_copy(which, to, send_sem):
+        return remote(all_queries.at[which], all_queries.at[which], send_sem, query_recv.at[which], to)
+
+    def send_queries(k, _):
+        query_copy(me, device((z + k) % depth, y, core), query_send.at[k]).start()
+        return 0
+
+    lax.fori_loop(1, depth, send_queries, 0)
+    query_copy(me, across, query_send.at[depth]).start()
+    query_copy(me, sibling, query_send.at[0]).start()
+
     table_copy.wait()
     grads_copy.wait()
     for i in range(V_PIECES):
@@ -226,8 +225,7 @@
         query_copy(which, across, pass_near.at[k]).start()
         query_copy(which, sibling, pass_far.at[k]).start()
 
-    lax.fori_loop(0, 2 * depth, for_sibling, 0)
-    pass_one(1)
+    lax.fori_loop(0, depth, for_sibling, 0)
 
     def for_near(k, _):
         total = partial(device((z + 1 + k) % depth, 1 - y, core))
@@ -237,7 +235,8 @@
         return 0
 
     lax.fori_loop(0, depth, for_near, 0)
-    for k in range(2, depth - 1):
+    lax.fori_loop(depth, 2 * depth, for_sibling, 0)
+    for k in range(1, depth):
         pass_one(k)
 
     def for_far(k):
@@ -252,7 +251,6 @@
         return 0
 
     lax.fori_loop(0, depth - 1, send_far, 0)
-    pass_one(depth - 1)
     features = for_far(depth - 1)
 
     def pass_across(k, _):

time: 32.1 us -> 30 us (0.935)
  Pallas kernels: 29.9 us -> 27.9 us
    pallas_call x1, Pallas kernels: 29.9 us -> 27.9 us  [fused_shards(): pl.pallas_call(functools.partial(fused_kernel, n), out_shape=jax.ShapeDty...]
where the time goes in v3:
time: 30 us; the launch traced here: 29.8 us
  Pallas kernels  27.9 us (93%)
  local copies, waits for them, and re-layouts  1.28 us (4%)
  between operations  0.66 us (2%)
    pallas_call x1, Pallas kernels, fused_shards(): pl.pallas_call(functools.partial(fused_kernel, n), out_shape=jax.ShapeDty...  27.9 us
    unnamed x1, local copies, waits for them, and re-layouts  1.28 us

profile of v3, /device:TPU:0, one launch (start us, length us, event | category | flops | bytes accessed | tf_op | source)
XLA Modules:
  0.0 29.8 jit_solution(14099991510426965481)
XLA Ops:
  0.7 27.9 %shard_map.73 = f32[6,128]{1,0:T(8,128)} custom-call(s32[2,128]{1,0:T(2,128)} %bitcast.2, s32[2,128]{1,0:T(2,128)} %bitcast.3, s32[1]{0:T(128)S(6)} %copy.9.counts, bf16[96,2048]{1,0:T(8,128)(2,1)} %grads_hbm.1, bf16[256,128,128]{2,1,0:T(8,128)(2,1)} %values_hbm.1, bf16[256,4096]{1,0:T(8,128)(2,1)} %gram_hbm.1, bf16[8,4096]{1,0:T(8,128)(2,1)} %queries.1), custom_call_target="tpu_custom_call" | custom-call | tf_op jit(solution)/shard_map/pallas_call | solution.py:355
  28.6 1.3 %copy.10 = f32[6,128]{1,0:T(8,128)} copy(f32[6,128]{1,0:T(8,128)} %shard_map.73) | data formatting | bytes 6144

commit v4 on v3

--- a/solution.py
+++ b/solution.py
@@ -261,24 +261,10 @@
 
     lax.fori_loop(0, depth, pass_across, 0)
 
-    def wait_passed(k, _):
-        query_copy(2 * k + 1 - core, sibling, query_send.at[0]).wait_recv()
-        return 0
-
-    lax.fori_loop(0, 2 * depth, wait_passed, 0)
-    gram_copy.wait()
-
-    stacked = all_queries[...].reshape(n * 2 * query_rows, half)
-    contract = (((1,), (1,)), ((), ()))
-    first = lax.dot_general(gram[:, :half], stacked, contract, preferred_element_type=jnp.float32)
-    second = lax.dot_general(gram[:, half:], stacked, contract, preferred_element_type=jnp.float32)
     across_all = n * 2 * query_rows
-    whitened = (first + pltpu.roll(second, across_all - query_rows, 1)).astype(jnp.bfloat16)
     row = lax.broadcasted_iota(jnp.int32, (across_all, n * query_rows), 0)
     col = lax.broadcasted_iota(jnp.int32, (across_all, n * query_rows), 1)
     pick = (row == (col // query_rows) * (2 * query_rows) + col % query_rows).astype(jnp.bfloat16)
-    whitened = jnp.dot(whitened, pick, preferred_element_type=jnp.float32).astype(jnp.bfloat16)
-
     for k in range(depth - 1):
         far_copy(k).wait_recv()
         features += far_in[k].astype(jnp.float32)
@@ -286,6 +272,21 @@
     rest = features - high.astype(jnp.float32)
     middle = rest.astype(jnp.bfloat16)
     low = (rest - middle.astype(jnp.float32)).astype(jnp.bfloat16)
+
+    def wait_passed(k, _):
+        query_copy(2 * k + 1 - core, sibling, query_send.at[0]).wait_recv()
+        return 0
+
+    lax.fori_loop(0, 2 * depth, wait_passed, 0)
+    gram_copy.wait()
+
+    stacked = all_queries[...].reshape(n * 2 * query_rows, half)
+    contract = (((1,), (1,)), ((), ()))
+    first = lax.dot_general(gram[:, :half], stacked, contract, preferred_element_type=jnp.float32)
+    second = lax.dot_general(gram[:, half:], stacked, contract, preferred_element_type=jnp.float32)
+    whitened = (first + pltpu.roll(second, across_all - query_rows, 1)).astype(jnp.bfloat16)
+    whitened = jnp.dot(whitened, pick, preferred_element_type=jnp.float32).astype(jnp.bfloat16)
+
     scores = jnp.dot(high, whitened, preferred_element_type=jnp.float32)
     scores += jnp.dot(middle, whitened, preferred_element_type=jnp.float32)
     scores += jnp.dot(low, whitened, preferred_element_type=jnp.float32)
@@ -301,34 +302,35 @@
         return 0
 
     lax.fori_loop(1, n, send_scores, 0)
+
+    def drain_pair(k, _):
+        pair_copy(k).wait_send()
+        return 0
+
+    lax.fori_loop(0, 2 * depth, drain_pair, 0)
+
+    def drain_depth(k, _):
+        near_copy(k).wait_send()
+        query_copy(me, sibling, query_send.at[k]).wait_send()
+        query_copy(me, sibling, pass_pair.at[k]).wait_send()
+        return 0
+
+    lax.fori_loop(0, depth, drain_depth, 0)
+    query_copy(me, sibling, query_send.at[depth]).wait_send()
+
+    def drain_far(k, _):
+        far_copy(k).wait_send()
+        query_copy(me, sibling, pass_near.at[k + 1]).wait_send()
+        query_copy(me, sibling, pass_far.at[k + 1]).wait_send()
+        return 0
+
+    lax.fori_loop(0, depth - 1, drain_far, 0)
+
     result = score_out[me]
     for k in range(1, n):
         score_copy(k).wait_recv()
         result += score_in[k]
     out[...] = result[:out_rows]
-
-    def drain_pair(k, _):
-        pair_copy(k).wait_send()
-        return 0
-
-    lax.fori_loop(0, 2 * depth, drain_pair, 0)
-
-    def drain_depth(k, _):
-        near_copy(k).wait_send()
-        query_copy(me, sibling, query_send.at[k]).wait_send()
-        query_copy(me, sibling, pass_pair.at[k]).wait_send()
-        return 0
-
-    lax.fori_loop(0, depth, drain_depth, 0)
-    query_copy(me, sibling, query_send.at[depth]).wait_send()
-
-    def drain_far(k, _):
-        far_copy(k).wait_send()
-        query_copy(me, sibling, pass_near.at[k + 1]).wait_send()
-        query_copy(me, sibling, pass_far.at[k + 1]).wait_send()
-        return 0
-
-    lax.fori_loop(0, depth - 1, drain_far, 0)
 
     def drain_scores(k, _):
         score_copy(k).wait_send()

time: 30 us -> 29.9 us (level)
  no operation moved by 1% of the time
where the time goes in v4:
time: 29.9 us; the launch traced here: 29.7 us
  Pallas kernels  27.8 us (93%)
  local copies, waits for them, and re-layouts  1.28 us (4%)
  between operations  0.66 us (2%)
    pallas_call x1, Pallas kernels, fused_shards(): pl.pallas_call(functools.partial(fused_kernel, n), out_shape=jax.ShapeDty...  27.8 us
    unnamed x1, local copies, waits for them, and re-layouts  1.28 us

profile of v4, /device:TPU:0, one launch (start us, length us, event | category | flops | bytes accessed | tf_op | source)
XLA Modules:
  0.0 29.7 jit_solution(14829548083130316791)
XLA Ops:
  0.7 27.8 %shard_map.73 = f32[6,128]{1,0:T(8,128)} custom-call(s32[2,128]{1,0:T(2,128)} %bitcast.2, s32[2,128]{1,0:T(2,128)} %bitcast.3, s32[1]{0:T(128)S(6)} %copy.9.counts, bf16[96,2048]{1,0:T(8,128)(2,1)} %grads_hbm.1, bf16[256,128,128]{2,1,0:T(8,128)(2,1)} %values_hbm.1, bf16[256,4096]{1,0:T(8,128)(2,1)} %gram_hbm.1, bf16[8,4096]{1,0:T(8,128)(2,1)} %queries.1), custom_call_target="tpu_custom_call" | custom-call | tf_op jit(solution)/shard_map/pallas_call | solution.py:357
  28.4 1.3 %copy.10 = f32[6,128]{1,0:T(8,128)} copy(f32[6,128]{1,0:T(8,128)} %shard_map.73) | data formatting | bytes 6144

commit v5 on v4

--- a/solution.py
+++ b/solution.py
@@ -101,6 +101,7 @@
     pair_send, pair_recv, near_send, near_recv, far_send, far_recv, score_send, score_recv,
 ):
     depth = n // 4
+    chips = n // 2
     me = lax.axis_index("blk")
     z, y, core = me // 4, (me // 2) % 2, me % 2
 
@@ -291,17 +292,29 @@
     scores += jnp.dot(middle, whitened, preferred_element_type=jnp.float32)
     scores += jnp.dot(low, whitened, preferred_element_type=jnp.float32)
     for d in range(n):
-        score_out[d, :out_rows, :] = scores[d * out_rows : (d + 1) * out_rows]
+        score_out[(d % 2) * chips + d // 2, :out_rows, :] = scores[d * out_rows : (d + 1) * out_rows]
+
+    theirs = pl.ds((1 - core) * chips, chips)
+    ours = pl.ds(core * chips, chips)
+    pair_scores = remote(
+        score_out.at[theirs], score_in.at[pl.ds(0, chips)], score_send.at[0], score_recv.at[0], sibling
+    )
+    pair_scores.start()
+    pair_scores.wait_recv()
+    score_out[ours] = score_out[ours] + score_in[:chips]
 
     def score_copy(k):
-        to = (me + k) % n
-        return remote(score_out.at[to], score_in.at[k], score_send.at[k], score_recv.at[k], to)
+        to = (me // 2 + k) % chips
+        return remote(
+            score_out.at[core * chips + to], score_in.at[chips + k],
+            score_send.at[k], score_recv.at[k], 2 * to + core,
+        )
 
     def send_scores(k, _):
         score_copy(k).start()
         return 0
 
-    lax.fori_loop(1, n, send_scores, 0)
+    lax.fori_loop(1, chips, send_scores, 0)
 
     def drain_pair(k, _):
         pair_copy(k).wait_send()
@@ -326,17 +339,18 @@
 
     lax.fori_loop(0, depth - 1, drain_far, 0)
 
-    result = score_out[me]
-    for k in range(1, n):
+    result = score_out[core * chips + me // 2]
+    for k in range(1, chips):
         score_copy(k).wait_recv()
-        result += score_in[k]
+        result += score_in[chips + k]
     out[...] = result[:out_rows]
 
     def drain_scores(k, _):
         score_copy(k).wait_send()
         return 0
 
-    lax.fori_loop(1, n, drain_scores, 0)
+    lax.fori_loop(1, chips, drain_scores, 0)
+    pair_scores.wait_send()
 
 
 def fused_shards(grads, block_values, block_rows, block_cols, block_counts, inv_gram, queries):

time: 29.9 us -> 31.2 us (1.043)
  Pallas kernels: 27.8 us -> 29.1 us
    pallas_call x1, Pallas kernels: 27.8 us -> 29.1 us  [fused_shards(): pl.pallas_call(functools.partial(fused_kernel, n), out_shape=jax.ShapeDty...]
where the time goes in v5:
time: 31.2 us; the launch traced here: 31 us
  Pallas kernels  29.1 us (93%)
  local copies, waits for them, and re-layouts  1.28 us (4%)
  between operations  0.66 us (2%)
    pallas_call x1, Pallas kernels, fused_shards(): pl.pallas_call(functools.partial(fused_kernel, n), out_shape=jax.ShapeDty...  29.1 us
    unnamed x1, local copies, waits for them, and re-layouts  1.28 us

profile of v5, /device:TPU:0, one launch (start us, length us, event | category | flops | bytes accessed | tf_op | source)
XLA Modules:
  0.0 31.0 jit_solution(15924416307706627417)
XLA Ops:
  0.7 29.1 %shard_map.73 = f32[6,128]{1,0:T(8,128)} custom-call(s32[2,128]{1,0:T(2,128)} %bitcast.2, s32[2,128]{1,0:T(2,128)} %bitcast.3, s32[1]{0:T(128)S(6)} %copy.9.counts, bf16[96,2048]{1,0:T(8,128)(2,1)} %grads_hbm.1, bf16[256,128,128]{2,1,0:T(8,128)(2,1)} %values_hbm.1, bf16[256,4096]{1,0:T(8,128)(2,1)} %gram_hbm.1, bf16[8,4096]{1,0:T(8,128)(2,1)} %queries.1), custom_call_target="tpu_custom_call" | custom-call | tf_op jit(solution)/shard_map/pallas_call | solution.py:371
  29.7 1.3 %copy.10 = f32[6,128]{1,0:T(8,128)} copy(f32[6,128]{1,0:T(8,128)} %shard_map.73) | data formatting | bytes 6144
